TPU v7x, 256 devices: a whole 4x4x8 slice. The times are simulated.
256 devices in a mesh: seq: 64 (over z, x, core), tp: 4 (over y).
Axes of the slice: x: 4, y: 4, z: 8, core: 2. Of those that a mesh axis runs over, the one named last changes fastest.
Arguments:
- tokens: bfloat16 [32768, 4096], P('seq', 'tp'), may hold values from -6 to 6
- log_decay: float32 [32768, 16], P('seq', 'tp'), may hold values from -2 to 0
- w_query: bfloat16 [4096, 2048], P(None, 'tp'), may hold values from -0.09375 to 0.09375
- w_key: bfloat16 [4096, 512], P(None, 'tp'), may hold values from -0.09375 to 0.09375
- w_value: bfloat16 [4096, 512], P(None, 'tp'), may hold values from -0.09375 to 0.09375
- w_level: bfloat16 [4096, 144], P(None, 'tp'), may hold values from -0.09375 to 0.09375
- w_out: bfloat16 [2048, 4096], P('tp'), may hold values from -0.125 to 0.125
Outputs:
- mixed: bfloat16 [32768, 4096], P('seq', 'tp')
All inputs are finite; a program needn't handle non-finite values.
Results may differ from a plain program's by a relative error of at most 0.02.
Values may be sent and summed in bfloat16 or wider, within the bound.
A program may use at most 128 MiB of HBM per device.

v0:
```python
import jax
import jax.numpy as jnp
from jax import lax
from jax.sharding import PartitionSpec as P

BLOCK = 128
HIGHEST = lax.Precision.HIGHEST
F32 = jnp.float32
BF16 = jnp.bfloat16


def body(tokens, log_decay, w_query, w_key, w_value, w_level, w_out):
    rows = tokens.shape[0]
    heads = log_decay.shape[1]
    size = w_out.shape[0] // heads
    level_count = w_level.shape[1] // heads
    blocks = rows // BLOCK
    local_bits = blocks.bit_length() - 1
    seq_size = lax.axis_size("seq")
    seq_bits = seq_size.bit_length() - 1
    device = lax.axis_index("seq")
    positions = jnp.arange(rows, dtype=jnp.int32)
    triangle = (positions[:, None] >= positions[None, :]).astype(F32)
    decay = jnp.dot(triangle, log_decay, precision=HIGHEST)
    total = decay[rows - 1]

    def swap(x, bit):
        pairs = [(i, i ^ 1 << bit) for i in range(seq_size)]
        return lax.ppermute(x, "seq", pairs)

    group, before = (total, jnp.zeros_like(total))
    befores, fades = ([], [])
    for bit in range(seq_bits):
        upper = jnp.right_shift(device, bit) & 1 == 1
        other = swap(group, bit)
        befores.append(jnp.where(upper, before, -jnp.inf))
        fades.append(jnp.exp(jnp.where(upper, group, other)))
        before = before + jnp.where(upper, other, 0.0)
        group = group + other
    piece = lax.all_gather(tokens, "tp", axis=1, tiled=True)
    dot = lambda a, b: jnp.dot(a, b, preferred_element_type=F32)
    keys = dot(piece, w_key).astype(BF16)
    values = dot(piece, w_value).astype(BF16)
    keep = jnp.exp(total[None, :] - decay)
    weighted = (keep.T[:, :, None] * keys.astype(F32)[None]).astype(BF16)
    state = jnp.einsum("htd,te->hde", weighted, values, preferred_element_type=F32)
    buckets = []
    for bit in range(seq_bits):
        upper = jnp.right_shift(device, bit) & 1 == 1
        other = swap(state.astype(BF16), bit)
        buckets.append(other)
        wide = other.astype(F32)
        low = jnp.where(upper, wide, state)
        high = jnp.where(upper, state, wide)
        state = high + fades[bit][:, None, None] * low
    query = dot(piece, w_query).astype(BF16).reshape(rows, heads, size)
    level = jax.nn.softplus(dot(piece, w_level)).reshape(rows, heads, level_count)
    qb = query.reshape(blocks, BLOCK, heads, size)
    kb = keys.reshape(blocks, BLOCK, size)
    vb = values.reshape(blocks, BLOCK, size)
    lb = level.reshape(blocks, BLOCK, heads, level_count)
    db = decay.reshape(blocks, BLOCK, heads)
    scores = jnp.einsum("cihd,cjd->hcij", qb, kb, preferred_element_type=F32)
    inside = jnp.arange(BLOCK)
    causal = inside[:, None] >= inside[None, :]
    dh = db.transpose(2, 0, 1)
    gaps = jnp.where(causal, dh[:, :, :, None] - dh[:, :, None, :], -jnp.inf)
    mixing = lb[:, :, :, 0].transpose(2, 0, 1)[:, :, :, None] * jnp.exp(gaps) * scores
    out = jnp.einsum("hcij,cje->hcie", mixing.astype(BF16), vb, preferred_element_type=F32)
    ends = db[:, BLOCK - 1]
    weighted = jnp.exp(ends[:, None] - db).transpose(2, 0, 1)[..., None] * kb.astype(F32)[None]
    small = jnp.einsum("hcjd,cje->hcde", weighted.astype(BF16), vb, preferred_element_type=F32)
    small_ends = ends
    parts = [out[:, c] for c in range(blocks)]
    for bit in range(local_bits):
        for c in range(blocks):
            if c >> bit & 1:
                s = (c >> bit) - 1
                factor = lb[c, :, :, 1 + bit] * jnp.exp(db[c] - small_ends[s][None, :])
                got = jnp.einsum(
                    "ihd,hde->hie", qb[c], small[:, s].astype(BF16), preferred_element_type=F32
                )
                parts[c] = parts[c] + factor.T[:, :, None] * got
        fade = jnp.exp(small_ends[1::2] - small_ends[0::2])
        small = small[:, 1::2] + fade.T[:, :, None, None] * small[:, 0::2]
        small_ends = small_ends[1::2]
    combined = jnp.concatenate(parts, axis=1)
    for bit in range(seq_bits):
        factor = level[:, :, 1 + local_bits + bit] * jnp.exp(decay + befores[bit][None, :])
        got = jnp.einsum("thd,hde->hte", query, buckets[bit], preferred_element_type=F32)
        combined = combined + factor.T[:, :, None] * got
    normed = (
        combined * lax.rsqrt(jnp.mean(combined * combined, axis=-1, keepdims=True) + 1e-05)
    ).astype(BF16)
    wide = normed.transpose(1, 0, 2).reshape(rows, heads * size)
    partial = dot(wide, w_out)
    return lax.psum_scatter(partial.astype(BF16), "tp", scatter_dimension=1, tiled=True)


def solution(mesh):
    in_specs = (
        P("seq", "tp"),
        P("seq", "tp"),
        P(None, "tp"),
        P(None, "tp"),
        P(None, "tp"),
        P(None, "tp"),
        P("tp", None),
    )
    return jax.shard_map(
        body, mesh=mesh, in_specs=in_specs, out_specs=P("seq", "tp"), check_vma=False
    )
```

profile of v0, /device:TPU:1, one launch (start us, length us, event | category | flops | bytes accessed | tf_op | source)
XLA Modules:
  0.0 197.4 jit_solution(4253804932975548665)
XLA Ops:
  8.7 3.3 %collective-permute-start.1 = (f32[4]{0:T(128)S(1)}, f32[4]{0:T(128)S(1)}, u32[]{:S(2)}, u32[]{:S(2)}) collective-permute-start(f32[4]{0:T(128)S(1)} %slice_reduce_fusion), channel_id=1, source_target_pairs={{0,4},{4,0},{8,12},{12,8},{16,20},{20,16},{24,28},{28,24},{32,36},... | collective-permute-start | bytes 56 | tf_op jit(solution)/shard_map/ppermute | solution.py:29
  16.2 2.4 %collective-permute-done.3 = f32[4]{0:T(128)S(1)} collective-permute-done((f32[4]{0:T(128)S(1)}, f32[4]{0:T(128)S(1)}, u32[]{:S(2)}, u32[]{:S(2)}) %collective-permute-start.3) | collective-permute-done | bytes 48 | tf_op jit(solution)/shard_map/ppermute | solution.py:29
  20.2 2.9 %collective-permute-done.5 = f32[4]{0:T(128)S(1)} collective-permute-done((f32[4]{0:T(128)S(1)}, f32[4]{0:T(128)S(1)}, u32[]{:S(2)}, u32[]{:S(2)}) %collective-permute-start.5) | collective-permute-done | bytes 48 | tf_op jit(solution)/shard_map/ppermute | solution.py:29
  23.6 2.4 %collective-permute-done.7 = f32[4]{0:T(128)S(1)} collective-permute-done((f32[4]{0:T(128)S(1)}, f32[4]{0:T(128)S(1)}, u32[]{:S(2)}, u32[]{:S(2)}) %collective-permute-start.7) | collective-permute-done | bytes 48 | tf_op jit(solution)/shard_map/ppermute | solution.py:29
  26.6 1.4 collective-permute-start.9
  28.0 1.9 collective-permute-done.9
  30.5 33.4 %all-gather.2.cloned.1.call-done = bf16[512,4096]{1,0:T(8,128)(2,1)} async-done(((bf16[512,1024]{1,0:T(8,128)(2,1)}), bf16[512,4096]{1,0:T(8,128)(2,1)}) %all-gather.2.cloned.1.call-update) | async-done | bytes 4194320 | tf_op jit(solution)/shard_map/all_gather | solution.py:40
  63.9 3.6 %compare_select_fusion = f32[512,36]{0,1:T(8,128)S(1)} fusion(bf16[512,4096]{1,0:T(8,128)(2,1)} %all-gather.2.cloned.1.call-done, bf16[4096,36]{0,1:T(8,128)(2,1)} %param.12), kind=kOutput, calls=%fused_computation.79 | convolution fusion | flops 151105536 | bytes 4562944 | tf_op jit(solution)/shard_map/dot_general | solution.py:41
  68.2 5.8 %convolution_convert_fusion.1 = bf16[512,512]{0,1:T(8,128)(2,1)S(1)} fusion(bf16[512,4096]{1,0:T(8,128)(2,1)} %all-gather.2.cloned.1.call-done, bf16[4096,512]{1,0:T(8,128)(2,1)} %param.9), kind=kOutput, calls=%fused_computation.17 | convolution fusion | flops 2147745792 | bytes 8912896 | tf_op jit(solution)/shard_map/dot_general | solution.py:41
  76.2 3.4 %convolution_convert_fusion.2 = bf16[512,128]{1,0:T(8,128)(2,1)S(1)} fusion(bf16[512,4096]{1,0:T(8,128)(2,1)} %all-gather.2.cloned.1.call-done, bf16[4096,128]{1,0:T(8,128)(2,1)S(1)} %copy-done), kind=kOutput, calls=%fused_computation.27 | convolution fusion | flops 536936448 | bytes 5373952 | tf_op jit(solution)/shard_map/dot_general | solution.py:41
  79.8 3.7 %convolution_convert_fusion.3 = bf16[512,128]{1,0:T(8,128)(2,1)S(1)} fusion(bf16[512,4096]{1,0:T(8,128)(2,1)} %all-gather.2.cloned.1.call-done, bf16[4096,128]{1,0:T(8,128)(2,1)} %param.11), kind=kOutput, calls=%fused_computation.28 | convolution fusion | flops 536936448 | bytes 5373952 | tf_op jit(solution)/shard_map/dot_general | solution.py:41
  88.4 2.8 %convolution_bitcast_fusion.1 = f32[4,4,128,128]{3,2,0,1:T(8,128)} fusion(bf16[4,128,128,1]{2,1,3,0:T(8,128)(2,1)} %bitcast.198, bf16[4,128,128,1]{2,1,3,0:T(8,128)(2,1)S(1)} %bitcast.194, bf16[4,128,4,128]{1,0,3,2:T(4,128)(2,1)S(1)} %reshape_reshape.7, f32[4,4,128]{2,0,1:T(4,128)} %copy.55, f32[4,4,128]{2,0,1:T(4,128)} %copy.54, ...), kind=kOutput, calls=%fused_computation.14 | convolution fusion | flops 135528448 | bytes 1867776 | tf_op jit(solution)/shard_map/hcij,cje->hcie/dot_general | solution.py:69
  96.8 1.3 collective-permute-start.2
  99.0 3.0 %collective-permute-done.2 = bf16[4,128,128]{2,1,0:T(8,128)(2,1)S(1)} collective-permute-done((bf16[4,128,128]{2,1,0:T(8,128)(2,1)S(1)}, bf16[4,128,128]{2,1,0:T(8,128)(2,1)S(1)}, u32[]{:S(2)}, u32[]{:S(2)}) %collective-permute-start.2) | collective-permute-done | bytes 131104 | tf_op jit(solution)/shard_map/ppermute | solution.py:29
  102.8 2.8 %collective-permute-start.4 = (bf16[4,128,128]{2,1,0:T(8,128)(2,1)S(1)}, bf16[4,128,128]{2,1,0:T(8,128)(2,1)S(1)}, u32[]{:S(2)}, u32[]{:S(2)}) collective-permute-start(bf16[4,128,128]{2,1,0:T(8,128)(2,1)S(1)} %fusion.43), channel_id=1, source_target_pairs={{0,16},{4,20},{8,24},{12,28},{16,0},{20,4},{24,8},{28,12},{32,48},... | collective-permute-start | bytes 393224 | tf_op jit(solution)/shard_map/ppermute | solution.py:29
  106.1 2.5 %collective-permute-done.4 = bf16[4,128,128]{2,1,0:T(8,128)(2,1)S(1)} collective-permute-done((bf16[4,128,128]{2,1,0:T(8,128)(2,1)S(1)}, bf16[4,128,128]{2,1,0:T(8,128)(2,1)S(1)}, u32[]{:S(2)}, u32[]{:S(2)}) %collective-permute-start.4) | collective-permute-done | bytes 131104 | tf_op jit(solution)/shard_map/ppermute | solution.py:29
  108.9 1.4 collective-permute-start.6
  110.8 2.0 %collective-permute-done.6 = bf16[4,128,128]{2,1,0:T(8,128)(2,1)S(1)} collective-permute-done((bf16[4,128,128]{2,1,0:T(8,128)(2,1)S(1)}, bf16[4,128,128]{2,1,0:T(8,128)(2,1)S(1)}, u32[]{:S(2)}, u32[]{:S(2)}) %collective-permute-start.6) | collective-permute-done | bytes 131104 | tf_op jit(solution)/shard_map/ppermute | solution.py:29
  112.9 2.3 %collective-permute-start.8 = (bf16[4,128,128]{2,1,0:T(8,128)(2,1)S(1)}, bf16[4,128,128]{2,1,0:T(8,128)(2,1)S(1)}, u32[]{:S(2)}, u32[]{:S(2)}) collective-permute-start(bf16[4,128,128]{2,1,0:T(8,128)(2,1)S(1)} %fusion.42), channel_id=1, source_target_pairs={{0,64},{4,68},{8,72},{12,76},{16,80},{20,84},{24,88},{28,92},{32,9... | collective-permute-start | bytes 393224 | tf_op jit(solution)/shard_map/ppermute | solution.py:29
  115.8 3.4 %collective-permute-done.8 = bf16[4,128,128]{2,1,0:T(8,128)(2,1)S(1)} collective-permute-done((bf16[4,128,128]{2,1,0:T(8,128)(2,1)S(1)}, bf16[4,128,128]{2,1,0:T(8,128)(2,1)S(1)}, u32[]{:S(2)}, u32[]{:S(2)}) %collective-permute-start.8) | collective-permute-done | bytes 131104 | tf_op jit(solution)/shard_map/ppermute | solution.py:29
  119.3 5.5 %collective-permute-start.10 = (bf16[4,128,128]{2,1,0:T(8,128)(2,1)S(1)}, bf16[4,128,128]{2,1,0:T(8,128)(2,1)S(1)}, u32[]{:S(2)}, u32[]{:S(2)}) collective-permute-start(bf16[4,128,128]{2,1,0:T(8,128)(2,1)S(1)} %fusion.39), channel_id=1, source_target_pairs={{0,128},{4,132},{8,136},{12,140},{16,144},{20,148},{24,152},{28,15... | collective-permute-start | bytes 393224 | tf_op jit(solution)/shard_map/ppermute | solution.py:29
  125.3 2.0 collective-permute-done.10
  129.5 6.5 %convolution_convert_fusion = bf16[512,4096]{1,0:T(8,128)(2,1)} fusion(bf16[512,512]{0,1:T(8,128)(2,1)S(1)} %bitcast.190, bf16[512,4096]{1,0:T(8,128)(2,1)} %param.13), kind=kOutput, calls=%fused_computation | convolution fusion | flops 2149580800 | bytes 8912896 | tf_op jit(solution)/shard_map/dot_general | solution.py:41
  136.0 54.5 %reduce-scatter.2.cloned.1.call-done = bf16[512,1024]{1,0:T(8,128)(2,1)} async-done(((bf16[512,4096]{1,0:T(8,128)(2,1)}), bf16[512,1024]{1,0:T(8,128)(2,1)}) %reduce-scatter.2.cloned.1.call-update) | async-done | bytes 1048592 | tf_op jit(solution)/shard_map/reduce_scatter | solution.py:97
  (109 shorter events, 29.2 us)
Async XLA Ops:
  6.5 69.7 %copy-start = (bf16[4096,128]{1,0:T(8,128)(2,1)S(1)}, bf16[4096,128]{1,0:T(8,128)(2,1)}, u32[]{:S(2)}) copy-start(bf16[4096,128]{1,0:T(8,128)(2,1)} %param.10) | copy-start | bytes 3145732
  6.5 57.3 %all-gather.2.cloned.1.call-start = ((), (), s32[]{:S(2)}) async-start(), calls=%async_computation.1 | async-start | bytes 5242880 | tf_op jit(solution)/shard_map/all_gather | solution.py:40
  7.3 183.3 %reduce-scatter.2.cloned.1.call-start = ((), (), s32[]{:S(2)}) async-start(), calls=%async_computation.2 | async-start | bytes 5242880 | tf_op jit(solution)/shard_map/reduce_scatter | solution.py:97
  8.6 55.2 %copy-start.9 = (f32[4]{0:T(128)}, f32[4]{0:T(128)S(1)}, u32[]{:S(2)}) copy-start(f32[4]{0:T(128)S(1)} %slice_reduce_fusion) | copy-start | bytes 52
  8.7 6.9 %collective-permute-start.1 = (f32[4]{0:T(128)S(1)}, f32[4]{0:T(128)S(1)}, u32[]{:S(2)}, u32[]{:S(2)}) collective-permute-start(f32[4]{0:T(128)S(1)} %slice_reduce_fusion), channel_id=1, source_target_pairs={{0,4},{4,0},{8,12},{12,8},{16,20},{20,16},{24,28},{28,24},{32,36},... | collective-permute-start | bytes 56 | tf_op jit(solution)/shard_map/ppermute | solution.py:29
  16.2 2.4 %collective-permute-start.3 = (f32[4]{0:T(128)S(1)}, f32[4]{0:T(128)S(1)}, u32[]{:S(2)}, u32[]{:S(2)}) collective-permute-start(f32[4]{0:T(128)S(1)} %get-tuple-element.50), channel_id=1, source_target_pairs={{0,8},{4,12},{8,0},{12,4},{16,24},{20,28},{24,16},{28,20},{32,40},... | collective-permute-start | bytes 56 | tf_op jit(solution)/shard_map/ppermute | solution.py:29
  19.2 3.9 %collective-permute-start.5 = (f32[4]{0:T(128)S(1)}, f32[4]{0:T(128)S(1)}, u32[]{:S(2)}, u32[]{:S(2)}) collective-permute-start(f32[4]{0:T(128)S(1)} %get-tuple-element.55), channel_id=1, source_target_pairs={{0,16},{4,20},{8,24},{12,28},{16,0},{20,4},{24,8},{28,12},{32,48},... | collective-permute-start | bytes 56 | tf_op jit(solution)/shard_map/ppermute | solution.py:29
  23.6 2.4 %collective-permute-start.7 = (f32[4]{0:T(128)S(1)}, f32[4]{0:T(128)S(1)}, u32[]{:S(2)}, u32[]{:S(2)}) collective-permute-start(f32[4]{0:T(128)S(1)} %get-tuple-element.45), channel_id=1, source_target_pairs={{0,32},{4,36},{8,40},{12,44},{16,48},{20,52},{24,56},{28,60},{32,0... | collective-permute-start | bytes 56 | tf_op jit(solution)/shard_map/ppermute | solution.py:29
  26.6 3.3 %collective-permute-start.9 = (f32[4]{0:T(128)S(1)}, f32[4]{0:T(128)S(1)}, u32[]{:S(2)}, u32[]{:S(2)}) collective-permute-start(f32[4]{0:T(128)S(1)} %get-tuple-element.43), channel_id=1, source_target_pairs={{0,64},{4,68},{8,72},{12,76},{16,80},{20,84},{24,88},{28,92},{32,9... | collective-permute-start | bytes 56 | tf_op jit(solution)/shard_map/ppermute | solution.py:29
  87.5 8.5 %collective-permute-start = (bf16[4,128,128]{2,1,0:T(8,128)(2,1)}, bf16[4,128,128]{2,1,0:T(8,128)(2,1)S(1)}, u32[]{:S(2)}, u32[]{:S(2)}) collective-permute-start(bf16[4,128,128]{2,1,0:T(8,128)(2,1)} %get-tuple-element.57), channel_id=1, source_target_pairs={{0,4},{4,0},{8,12},{12,8},{16,20},{20,16},{24,28},{28,24},{32,36},... | collective-permute-start | bytes 393224 | tf_op jit(solution)/shard_map/ppermute | solution.py:29
  88.3 20.3 %copy-start.7 = (f32[4]{0:T(128)S(1)}, f32[4]{0:T(128)}, u32[]{:S(2)}) copy-start(f32[4]{0:T(128)} %get-tuple-element.49) | copy-start | bytes 52
  88.4 20.3 %copy-start.8 = (f32[4]{0:T(128)S(1)}, f32[4]{0:T(128)}, u32[]{:S(2)}) copy-start(f32[4]{0:T(128)} %get-tuple-element.56) | copy-start | bytes 52
  88.4 20.3 %copy-start.12 = (f32[4]{0:T(128)S(1)}, f32[4]{0:T(128)}, u32[]{:S(2)}) copy-start(f32[4]{0:T(128)} %get-tuple-element.46) | copy-start | bytes 52
  91.2 19.1 %copy-start.4 = (f32[4,512]{1,0:T(4,128)S(1)}, f32[4,512]{1,0:T(4,128)}, u32[]{:S(2)}) copy-start(f32[4,512]{1,0:T(4,128)} %get-tuple-element.32) | copy-start | bytes 24580
  93.2 19.6 %copy-start.11 = (f32[4]{0:T(128)S(1)}, f32[4]{0:T(128)}, u32[]{:S(2)}) copy-start(f32[4]{0:T(128)} %get-tuple-element.44) | copy-start | bytes 52
  93.4 21.8 %copy-start.3 = (f32[4,512]{1,0:T(4,128)S(1)}, f32[4,512]{1,0:T(4,128)}, u32[]{:S(2)}) copy-start(f32[4,512]{1,0:T(4,128)} %get-tuple-element.31) | copy-start | bytes 24580
  96.0 23.1 %copy-start.13 = (f32[4]{0:T(128)S(1)}, f32[4]{0:T(128)}, u32[]{:S(2)}) copy-start(f32[4]{0:T(128)} %get-tuple-element.53) | copy-start | bytes 52
  96.8 28.0 %copy-start.2 = (f32[4,512]{1,0:T(4,128)S(1)}, f32[4,512]{1,0:T(4,128)}, u32[]{:S(2)}) copy-start(f32[4,512]{1,0:T(4,128)} %get-tuple-element.30) | copy-start | bytes 24580
  96.8 5.2 %collective-permute-start.2 = (bf16[4,128,128]{2,1,0:T(8,128)(2,1)S(1)}, bf16[4,128,128]{2,1,0:T(8,128)(2,1)S(1)}, u32[]{:S(2)}, u32[]{:S(2)}) collective-permute-start(bf16[4,128,128]{2,1,0:T(8,128)(2,1)S(1)} %fusion.74), channel_id=1, source_target_pairs={{0,8},{4,12},{8,0},{12,4},{16,24},{20,28},{24,16},{28,20},{32,40},... | collective-permute-start | bytes 393224 | tf_op jit(solution)/shard_map/ppermute | solution.py:29
  102.8 5.8 %collective-permute-start.4 = (bf16[4,128,128]{2,1,0:T(8,128)(2,1)S(1)}, bf16[4,128,128]{2,1,0:T(8,128)(2,1)S(1)}, u32[]{:S(2)}, u32[]{:S(2)}) collective-permute-start(bf16[4,128,128]{2,1,0:T(8,128)(2,1)S(1)} %fusion.43), channel_id=1, source_target_pairs={{0,16},{4,20},{8,24},{12,28},{16,0},{20,4},{24,8},{28,12},{32,48},... | collective-permute-start | bytes 393224 | tf_op jit(solution)/shard_map/ppermute | solution.py:29
  108.9 18.9 %copy-start.6 = (f32[4,512]{1,0:T(4,128)S(1)}, f32[4,512]{1,0:T(4,128)}, u32[]{:S(2)}) copy-start(f32[4,512]{1,0:T(4,128)} %get-tuple-element.28) | copy-start | bytes 24580
  108.9 3.9 %collective-permute-start.6 = (bf16[4,128,128]{2,1,0:T(8,128)(2,1)S(1)}, bf16[4,128,128]{2,1,0:T(8,128)(2,1)S(1)}, u32[]{:S(2)}, u32[]{:S(2)}) collective-permute-start(bf16[4,128,128]{2,1,0:T(8,128)(2,1)S(1)} %get-tuple-element.9), channel_id=1, source_target_pairs={{0,32},{4,36},{8,40},{12,44},{16,48},{20,52},{24,56},{28,60},{32,0... | collective-permute-start | bytes 393224 | tf_op jit(solution)/shard_map/ppermute | solution.py:29
  112.9 6.2 %collective-permute-start.8 = (bf16[4,128,128]{2,1,0:T(8,128)(2,1)S(1)}, bf16[4,128,128]{2,1,0:T(8,128)(2,1)S(1)}, u32[]{:S(2)}, u32[]{:S(2)}) collective-permute-start(bf16[4,128,128]{2,1,0:T(8,128)(2,1)S(1)} %fusion.42), channel_id=1, source_target_pairs={{0,64},{4,68},{8,72},{12,76},{16,80},{20,84},{24,88},{28,92},{32,9... | collective-permute-start | bytes 393224 | tf_op jit(solution)/shard_map/ppermute | solution.py:29
  119.3 8.0 %collective-permute-start.10 = (bf16[4,128,128]{2,1,0:T(8,128)(2,1)S(1)}, bf16[4,128,128]{2,1,0:T(8,128)(2,1)S(1)}, u32[]{:S(2)}, u32[]{:S(2)}) collective-permute-start(bf16[4,128,128]{2,1,0:T(8,128)(2,1)S(1)} %fusion.39), channel_id=1, source_target_pairs={{0,128},{4,132},{8,136},{12,140},{16,144},{20,148},{24,152},{28,15... | collective-permute-start | bytes 393224 | tf_op jit(solution)/shard_map/ppermute | solution.py:29
  (10 other events, 68.4 us)
Sparse Core Ops, SparseCore 0:
  9.2 54.6 all-gather.1
  136.1 54.3 reduce-scatter.1
where the time goes:
time: 198 us; the launch traced here: 197 us
  waiting for transfers between devices  111 us (56%)
  matrix products  36.4 us (18%)
  starting transfers between devices  19.8 us (10%)
  between operations  13.9 us (7%)
  local copies, waits for them, and re-layouts  8.63 us (4%)
  other arithmetic  7.64 us (4%)
    reduce_scatter x1, waiting for transfers between devices, body(): lax.psum_scatter(partial.astype(BF16), 'tp', scatter_dimension=1, tiled=T...  54.5 us
    all_gather x1, waiting for transfers between devices, body(): piece = lax.all_gather(tokens, 'tp', axis=1, tiled=True)  33.4 us
    dot_general x5, matrix products, body(): dot = lambda a, b: jnp.dot(a, b, preferred_element_type=F32)  23.2 us
    ppermute x11, waiting for transfers between devices, swap(): return lax.ppermute(x, 'seq', pairs)  22.4 us
    ppermute x11, starting transfers between devices, swap(): return lax.ppermute(x, 'seq', pairs)  19.8 us
    dot_general x4, matrix products, body(): jnp.einsum('ihd,hde->hie', qb[c], small[:, s].astype(BF16), preferred_ele...  3.96 us
  transfers between devices with their start and end apart: 13, of which 11 were waited for; matrix products, arithmetic and copies ran while one was open for 9% of the time, Pallas kernels for 0%

commit v1 on v0

--- a/solution.py
+++ b/solution.py
@@ -7,6 +7,12 @@
 HIGHEST = lax.Precision.HIGHEST
 F32 = jnp.float32
 BF16 = jnp.bfloat16
+
+
+def in_order(blocks, dim):
+    blocks = jnp.moveaxis(blocks, 0, dim)
+    shape = blocks.shape
+    return blocks.reshape(*shape[:dim], shape[dim] * shape[dim + 1], *shape[dim + 2 :])
 
 
 def body(tokens, log_decay, w_query, w_key, w_value, w_level, w_out):
@@ -37,7 +43,19 @@
         fades.append(jnp.exp(jnp.where(upper, group, other)))
         before = before + jnp.where(upper, other, 0.0)
         group = group + other
-    piece = lax.all_gather(tokens, "tp", axis=1, tiled=True)
+    length = lax.axis_size("tp")
+    pairs_2 = [(i_2, (i_2 + 1) % length) for i_2 in range(length)]
+    back = [(b_2, a_2) for a_2, b_2 in pairs_2]
+    lower, upper_2 = ([], [])
+    for step in range(length - 1):
+        if step % 2 == 0:
+            lower.append(lax.ppermute(lower[-1] if lower else tokens, "tp", pairs_2))
+        else:
+            upper_2.append(lax.ppermute(upper_2[-1] if upper_2 else tokens, "tp", back))
+    pieces = jnp.stack([*lower[::-1], tokens, *upper_2])
+    shift = lax.axis_index("tp") - len(lower)
+    pieces = pieces[(jnp.arange(length) - shift) % length]
+    piece = in_order(pieces, 1)
     dot = lambda a, b: jnp.dot(a, b, preferred_element_type=F32)
     keys = dot(piece, w_key).astype(BF16)
     values = dot(piece, w_value).astype(BF16)

time: 198 us -> 207 us (1.045)
  waiting for transfers between devices: 111 us -> 88.2 us
  starting transfers between devices: 19.8 us -> 37.6 us
  local copies, waits for them, and re-layouts: 8.63 us -> 20.3 us
  other arithmetic: 7.64 us -> 11.4 us
    all_gather x1 -> x0, waiting for transfers between devices: 33.4 us -> none  [body(): piece = lax.all_gather(tokens, 'tp', axis=1, tiled=True)]
    ppermute x0 -> x3, waiting for transfers between devices: none -> 18.3 us  [the longest x2 18.3 us: body(): lower.append(lax.ppermute(lower[-1] if lower else tokens, 'tp', pairs_2))]
    ppermute x11, starting transfers between devices: 19.8 us -> 32.4 us  [swap(): return lax.ppermute(x, 'seq', pairs)]
    transpose x0 -> x1, local copies, waits for them, and re-layouts: none -> 6.23 us  [in_order(): blocks = jnp.moveaxis(blocks, 0, dim)]
    ppermute x11, waiting for transfers between devices: 22.4 us -> 16.9 us  [swap(): return lax.ppermute(x, 'seq', pairs)]
    ppermute x0 -> x3, starting transfers between devices: none -> 5.13 us  [the longest x2 3.69 us: body(): lower.append(lax.ppermute(lower[-1] if lower else tokens, 'tp', pairs_2))]
    gather x0 -> x1, local copies, waits for them, and re-layouts: none -> 5.04 us  [body(): pieces = pieces[(jnp.arange(length) - shift) % length]]
    another operation x0 -> x1, other arithmetic: none -> 3.32 us  [body(): pieces = jnp.stack([*lower[::-1], tokens, *upper_2])]
  transfers between devices with their start and end apart: 13 -> 15, of which waited for: 11 -> 12; matrix products, arithmetic and copies ran while one was open for 9% -> 9% of each run, Pallas kernels for 0% -> 0%
where the time goes in v1:
time: 207 us; the launch traced here: 206 us
  waiting for transfers between devices  88.2 us (43%)
  starting transfers between devices  37.6 us (18%)
  matrix products  34.7 us (17%)
  local copies, waits for them, and re-layouts  20.3 us (10%)
  between operations  13.8 us (7%)
  other arithmetic  11.4 us (6%)
    reduce_scatter x1, waiting for transfers between devices, body(): lax.psum_scatter(partial.astype(BF16), 'tp', scatter_dimension=1, tiled=T...  53 us
    ppermute x11, starting transfers between devices, swap(): return lax.ppermute(x, 'seq', pairs)  32.4 us
    dot_general x5, matrix products, body(): dot = lambda a, b: jnp.dot(a, b, preferred_element_type=F32)  21.7 us
    ppermute x2, waiting for transfers between devices, body(): lower.append(lax.ppermute(lower[-1] if lower else tokens, 'tp', pairs_2))  18.3 us
    ppermute x11, waiting for transfers between devices, swap(): return lax.ppermute(x, 'seq', pairs)  16.9 us
    transpose x1, local copies, waits for them, and re-layouts, in_order(): blocks = jnp.moveaxis(blocks, 0, dim)  6.23 us
    gather x1, local copies, waits for them, and re-layouts, body(): pieces = pieces[(jnp.arange(length) - shift) % length]  5.04 us
  transfers between devices with their start and end apart: 15, of which 12 were waited for; matrix products, arithmetic and copies ran while one was open for 9% of the time, Pallas kernels for 0%

profile of v1, /device:TPU:1, one launch (start us, length us, event | category | flops | bytes accessed | tf_op | source)
XLA Modules:
  0.0 205.9 jit_solution(3673473143288593350)
XLA Ops:
  6.5 2.1 %collective-permute-start = (bf16[512,1024]{1,0:T(8,128)(2,1)}, bf16[512,1024]{1,0:T(8,128)(2,1)S(1)}, u32[]{:S(2)}, u32[]{:S(2)}) collective-permute-start(bf16[512,1024]{1,0:T(8,128)(2,1)} %param.7), channel_id=1, source_target_pairs={{0,1},{1,2},{2,3},{3,0},{4,5},{5,6},{6,7},{7,4},{8,9},{9,10},{10,1... | collective-permute-start | bytes 3145736 | tf_op jit(solution)/shard_map/ppermute | solution.py:52
  11.5 3.0 %collective-permute-start.4 = (f32[4]{0:T(128)S(1)}, f32[4]{0:T(128)S(1)}, u32[]{:S(2)}, u32[]{:S(2)}) collective-permute-start(f32[4]{0:T(128)S(1)} %slice_reduce_fusion), channel_id=1, source_target_pairs={{0,4},{4,0},{8,12},{12,8},{16,20},{20,16},{24,28},{28,24},{32,36},... | collective-permute-start | bytes 56 | tf_op jit(solution)/shard_map/ppermute | solution.py:35
  18.5 12.6 %collective-permute-done = bf16[512,1024]{1,0:T(8,128)(2,1)S(1)} collective-permute-done((bf16[512,1024]{1,0:T(8,128)(2,1)}, bf16[512,1024]{1,0:T(8,128)(2,1)S(1)}, u32[]{:S(2)}, u32[]{:S(2)}) %collective-permute-start) | collective-permute-done | bytes 1048608 | tf_op jit(solution)/shard_map/ppermute | solution.py:52
  36.2 3.0 %collective-permute-start.8 = (f32[4]{0:T(128)S(1)}, f32[4]{0:T(128)S(1)}, u32[]{:S(2)}, u32[]{:S(2)}) collective-permute-start(f32[4]{0:T(128)S(1)} %get-tuple-element.55), channel_id=1, source_target_pairs={{0,16},{4,20},{8,24},{12,28},{16,0},{20,4},{24,8},{28,12},{32,48},... | collective-permute-start | bytes 56 | tf_op jit(solution)/shard_map/ppermute | solution.py:35
  44.3 3.0 %collective-permute-start.12 = (f32[4]{0:T(128)S(1)}, f32[4]{0:T(128)S(1)}, u32[]{:S(2)}, u32[]{:S(2)}) collective-permute-start(f32[4]{0:T(128)S(1)} %get-tuple-element.43), channel_id=1, source_target_pairs={{0,64},{4,68},{8,72},{12,76},{16,80},{20,84},{24,88},{28,92},{32,9... | collective-permute-start | bytes 56 | tf_op jit(solution)/shard_map/ppermute | solution.py:35
  49.1 5.6 %collective-permute-done.1 = bf16[512,1024]{1,0:T(8,128)(2,1)S(1)} collective-permute-done((bf16[512,1024]{1,0:T(8,128)(2,1)S(1)}, bf16[512,1024]{1,0:T(8,128)(2,1)S(1)}, u32[]{:S(2)}, u32[]{:S(2)}) %collective-permute-start.1) | collective-permute-done | bytes 1048608 | tf_op jit(solution)/shard_map/ppermute | solution.py:52
  54.8 3.3 %pad_maximum_fusion = bf16[4,512,1024]{2,1,0:T(8,128)(2,1)} fusion(bf16[1,512,1024]{2,1,0:T(8,128)(2,1)S(1)} %bitcast.208, bf16[1,512,1024]{2,1,0:T(8,128)(2,1)} %bitcast.206, bf16[1,512,1024]{2,1,0:T(8,128)(2,1)S(1)} %bitcast.207, bf16[1,512,1024]{2,1,0:T(8,128)(2,1)S(1)} %bitcast.209), kind=kLoop, calls=%fused_computation.2 | loop fusion | flops 6291456 | bytes 8388608 | tf_op jit(solution)/shard_map/stack | solution.py:55
  58.1 5.0 %gather_fusion = bf16[4,512,1024]{2,1,0:T(8,128)(2,1)} fusion(bf16[4,512,1024]{2,1,0:T(8,128)(2,1)} %pad_maximum_fusion, s32[1024]{0:T(1024)S(1)} %pad_clamp_fusion), kind=kCustom, calls=%fused_computation | custom fusion | bytes 8388624 | tf_op jit(solution)/shard_map/gather | solution.py:57
  63.1 6.2 %copy.101 = bf16[512,4,1024]{0,2,1:T(8,128)(2,1)} copy(bf16[512,4,1024]{2,0,1:T(8,128)(2,1)} %bitcast.202) | data formatting | bytes 8388608 | tf_op jit(solution)/shard_map/transpose | solution.py:13
  69.4 3.0 %compare_select_fusion = f32[512,36]{0,1:T(8,128)S(1)} fusion(bf16[512,4096]{0,1:T(8,128)(2,1)} %bitcast.198, bf16[4096,36]{0,1:T(8,128)(2,1)S(1)} %copy-done.3), kind=kOutput, calls=%fused_computation.81 | convolution fusion | flops 151105536 | bytes 4562944 | tf_op jit(solution)/shard_map/dot_general | solution.py:59
  73.0 5.8 %convolution_convert_fusion.1 = bf16[512,512]{0,1:T(8,128)(2,1)S(1)} fusion(bf16[512,4096]{0,1:T(8,128)(2,1)} %bitcast.199, bf16[4096,512]{1,0:T(8,128)(2,1)} %param.9), kind=kOutput, calls=%fused_computation.19 | convolution fusion | flops 2147745792 | bytes 8912896 | tf_op jit(solution)/shard_map/dot_general | solution.py:59
  81.0 3.8 %convolution_convert_fusion.2 = bf16[512,128]{1,0:T(8,128)(2,1)S(1)} fusion(bf16[512,4096]{0,1:T(8,128)(2,1)} %bitcast.200, bf16[4096,128]{1,0:T(8,128)(2,1)S(1)} %copy-done), kind=kOutput, calls=%fused_computation.29 | convolution fusion | flops 536936448 | bytes 5373952 | tf_op jit(solution)/shard_map/dot_general | solution.py:59
  84.8 2.5 %convolution_convert_fusion.3 = bf16[512,128]{1,0:T(8,128)(2,1)S(1)} fusion(bf16[512,4096]{0,1:T(8,128)(2,1)S(1)} %bitcast.201, bf16[4096,128]{1,0:T(8,128)(2,1)} %param.11), kind=kOutput, calls=%fused_computation.30 | convolution fusion | flops 536936448 | bytes 5373952 | tf_op jit(solution)/shard_map/dot_general | solution.py:59
  92.1 3.7 %collective-permute-start.3 = (bf16[4,128,128]{2,1,0:T(8,128)(2,1)}, bf16[4,128,128]{2,1,0:T(8,128)(2,1)S(1)}, u32[]{:S(2)}, u32[]{:S(2)}) collective-permute-start(bf16[4,128,128]{2,1,0:T(8,128)(2,1)} %get-tuple-element.57), channel_id=1, source_target_pairs={{0,4},{4,0},{8,12},{12,8},{16,20},{20,16},{24,28},{28,24},{32,36},... | collective-permute-start | bytes 393224 | tf_op jit(solution)/shard_map/ppermute | solution.py:35
  95.9 2.6 %convolution_bitcast_fusion.1 = f32[4,4,128,128]{3,2,0,1:T(8,128)} fusion(bf16[4,128,128,1]{2,1,3,0:T(8,128)(2,1)} %bitcast.215, bf16[4,128,128,1]{2,1,3,0:T(8,128)(2,1)S(1)} %bitcast.211, bf16[4,128,4,128]{1,0,3,2:T(4,128)(2,1)S(1)} %reshape_reshape.7, f32[4,4,128]{2,0,1:T(4,128)} %copy.103, f32[4,4,128]{2,0,1:T(4,128)} %copy.102, ...), kind=kOutput, calls=%fused_computation.16 | convolution fusion | flops 135528448 | bytes 1867776 | tf_op jit(solution)/shard_map/hcij,cje->hcie/dot_general | solution.py:87
  104.0 2.6 %collective-permute-start.5 = (bf16[4,128,128]{2,1,0:T(8,128)(2,1)S(1)}, bf16[4,128,128]{2,1,0:T(8,128)(2,1)S(1)}, u32[]{:S(2)}, u32[]{:S(2)}) collective-permute-start(bf16[4,128,128]{2,1,0:T(8,128)(2,1)S(1)} %fusion.76), channel_id=1, source_target_pairs={{0,8},{4,12},{8,0},{12,4},{16,24},{20,28},{24,16},{28,20},{32,40},... | collective-permute-start | bytes 393224 | tf_op jit(solution)/shard_map/ppermute | solution.py:35
  107.6 2.9 %collective-permute-done.5 = bf16[4,128,128]{2,1,0:T(8,128)(2,1)S(1)} collective-permute-done((bf16[4,128,128]{2,1,0:T(8,128)(2,1)S(1)}, bf16[4,128,128]{2,1,0:T(8,128)(2,1)S(1)}, u32[]{:S(2)}, u32[]{:S(2)}) %collective-permute-start.5) | collective-permute-done | bytes 131104 | tf_op jit(solution)/shard_map/ppermute | solution.py:35
  111.2 2.9 %collective-permute-start.7 = (bf16[4,128,128]{2,1,0:T(8,128)(2,1)S(1)}, bf16[4,128,128]{2,1,0:T(8,128)(2,1)S(1)}, u32[]{:S(2)}, u32[]{:S(2)}) collective-permute-start(bf16[4,128,128]{2,1,0:T(8,128)(2,1)S(1)} %fusion.43), channel_id=1, source_target_pairs={{0,16},{4,20},{8,24},{12,28},{16,0},{20,4},{24,8},{28,12},{32,48},... | collective-permute-start | bytes 393224 | tf_op jit(solution)/shard_map/ppermute | solution.py:35
  114.6 2.7 %collective-permute-done.7 = bf16[4,128,128]{2,1,0:T(8,128)(2,1)S(1)} collective-permute-done((bf16[4,128,128]{2,1,0:T(8,128)(2,1)S(1)}, bf16[4,128,128]{2,1,0:T(8,128)(2,1)S(1)}, u32[]{:S(2)}, u32[]{:S(2)}) %collective-permute-start.7) | collective-permute-done | bytes 131104 | tf_op jit(solution)/shard_map/ppermute | solution.py:35
  121.8 3.1 %collective-permute-start.11 = (bf16[4,128,128]{2,1,0:T(8,128)(2,1)S(1)}, bf16[4,128,128]{2,1,0:T(8,128)(2,1)S(1)}, u32[]{:S(2)}, u32[]{:S(2)}) collective-permute-start(bf16[4,128,128]{2,1,0:T(8,128)(2,1)S(1)} %fusion.42), channel_id=1, source_target_pairs={{0,64},{4,68},{8,72},{12,76},{16,80},{20,84},{24,88},{28,92},{32,9... | collective-permute-start | bytes 393224 | tf_op jit(solution)/shard_map/ppermute | solution.py:35
  125.3 3.3 %collective-permute-done.11 = bf16[4,128,128]{2,1,0:T(8,128)(2,1)S(1)} collective-permute-done((bf16[4,128,128]{2,1,0:T(8,128)(2,1)S(1)}, bf16[4,128,128]{2,1,0:T(8,128)(2,1)S(1)}, u32[]{:S(2)}, u32[]{:S(2)}) %collective-permute-start.11) | collective-permute-done | bytes 131104 | tf_op jit(solution)/shard_map/ppermute | solution.py:35
  128.7 6.2 %collective-permute-start.13 = (bf16[4,128,128]{2,1,0:T(8,128)(2,1)S(1)}, bf16[4,128,128]{2,1,0:T(8,128)(2,1)S(1)}, u32[]{:S(2)}, u32[]{:S(2)}) collective-permute-start(bf16[4,128,128]{2,1,0:T(8,128)(2,1)S(1)} %fusion.39), channel_id=1, source_target_pairs={{0,128},{4,132},{8,136},{12,140},{16,144},{20,148},{24,152},{28,15... | collective-permute-start | bytes 393224 | tf_op jit(solution)/shard_map/ppermute | solution.py:35
  139.5 6.6 %convolution_convert_fusion = bf16[512,4096]{1,0:T(8,128)(2,1)} fusion(bf16[512,512]{0,1:T(8,128)(2,1)S(1)} %bitcast.203, bf16[512,4096]{1,0:T(8,128)(2,1)} %param.13), kind=kOutput, calls=%fused_computation.1 | convolution fusion | flops 2149580800 | bytes 8912896 | tf_op jit(solution)/shard_map/dot_general | solution.py:59
  146.1 53.0 %reduce-scatter.2.cloned.1.call-done = bf16[512,1024]{1,0:T(8,128)(2,1)} async-done(((bf16[512,4096]{1,0:T(8,128)(2,1)}), bf16[512,1024]{1,0:T(8,128)(2,1)}) %reduce-scatter.2.cloned.1.call-update) | async-done | bytes 1048592 | tf_op jit(solution)/shard_map/reduce_scatter | solution.py:115
  (109 shorter events, 43.7 us)
Async XLA Ops:
  6.5 74.5 %copy-start = (bf16[4096,128]{1,0:T(8,128)(2,1)S(1)}, bf16[4096,128]{1,0:T(8,128)(2,1)}, u32[]{:S(2)}) copy-start(bf16[4096,128]{1,0:T(8,128)(2,1)} %param.10) | copy-start | bytes 3145732
  6.5 192.6 %reduce-scatter.2.cloned.1.call-start = ((), (), s32[]{:S(2)}) async-start(), calls=%async_computation.1 | async-start | bytes 5242880 | tf_op jit(solution)/shard_map/reduce_scatter | solution.py:115
  6.5 24.6 %collective-permute-start = (bf16[512,1024]{1,0:T(8,128)(2,1)}, bf16[512,1024]{1,0:T(8,128)(2,1)S(1)}, u32[]{:S(2)}, u32[]{:S(2)}) collective-permute-start(bf16[512,1024]{1,0:T(8,128)(2,1)} %param.7), channel_id=1, source_target_pairs={{0,1},{1,2},{2,3},{3,0},{4,5},{5,6},{6,7},{7,4},{8,9},{9,10},{10,1... | collective-permute-start | bytes 3145736 | tf_op jit(solution)/shard_map/ppermute | solution.py:52
  8.7 40.5 %collective-permute-start.2 = (bf16[512,1024]{1,0:T(8,128)(2,1)}, bf16[512,1024]{1,0:T(8,128)(2,1)S(1)}, u32[]{:S(2)}, u32[]{:S(2)}) collective-permute-start(bf16[512,1024]{1,0:T(8,128)(2,1)} %param.7), channel_id=1, source_target_pairs={{1,0},{2,1},{3,2},{0,3},{5,4},{6,5},{7,6},{4,7},{9,8},{10,9},{11,1... | collective-permute-start | bytes 3145736 | tf_op jit(solution)/shard_map/ppermute | solution.py:54
  11.4 46.6 %copy-start.11 = (f32[4]{0:T(128)}, f32[4]{0:T(128)S(1)}, u32[]{:S(2)}) copy-start(f32[4]{0:T(128)S(1)} %slice_reduce_fusion) | copy-start | bytes 52
  11.5 21.3 %collective-permute-start.4 = (f32[4]{0:T(128)S(1)}, f32[4]{0:T(128)S(1)}, u32[]{:S(2)}, u32[]{:S(2)}) collective-permute-start(f32[4]{0:T(128)S(1)} %slice_reduce_fusion), channel_id=1, source_target_pairs={{0,4},{4,0},{8,12},{12,8},{16,20},{20,16},{24,28},{28,24},{32,36},... | collective-permute-start | bytes 56 | tf_op jit(solution)/shard_map/ppermute | solution.py:35
  31.2 23.6 %collective-permute-start.1 = (bf16[512,1024]{1,0:T(8,128)(2,1)S(1)}, bf16[512,1024]{1,0:T(8,128)(2,1)S(1)}, u32[]{:S(2)}, u32[]{:S(2)}) collective-permute-start(bf16[512,1024]{1,0:T(8,128)(2,1)S(1)} %collective-permute-done), channel_id=1, source_target_pairs={{0,1},{1,2},{2,3},{3,0},{4,5},{5,6},{6,7},{7,4},{8,9},{9,10},{10,1... | collective-permute-start | bytes 3145736 | tf_op jit(solution)/shard_map/ppermute | solution.py:52
  33.3 2.4 %collective-permute-start.6 = (f32[4]{0:T(128)S(1)}, f32[4]{0:T(128)S(1)}, u32[]{:S(2)}, u32[]{:S(2)}) collective-permute-start(f32[4]{0:T(128)S(1)} %get-tuple-element.50), channel_id=1, source_target_pairs={{0,8},{4,12},{8,0},{12,4},{16,24},{20,28},{24,16},{28,20},{32,40},... | collective-permute-start | bytes 56 | tf_op jit(solution)/shard_map/ppermute | solution.py:35
  36.2 3.9 %collective-permute-start.8 = (f32[4]{0:T(128)S(1)}, f32[4]{0:T(128)S(1)}, u32[]{:S(2)}, u32[]{:S(2)}) collective-permute-start(f32[4]{0:T(128)S(1)} %get-tuple-element.55), channel_id=1, source_target_pairs={{0,16},{4,20},{8,24},{12,28},{16,0},{20,4},{24,8},{28,12},{32,48},... | collective-permute-start | bytes 56 | tf_op jit(solution)/shard_map/ppermute | solution.py:35
  40.7 3.1 %collective-permute-start.10 = (f32[4]{0:T(128)S(1)}, f32[4]{0:T(128)S(1)}, u32[]{:S(2)}, u32[]{:S(2)}) collective-permute-start(f32[4]{0:T(128)S(1)} %get-tuple-element.45), channel_id=1, source_target_pairs={{0,32},{4,36},{8,40},{12,44},{16,48},{20,52},{24,56},{28,60},{32,0... | collective-permute-start | bytes 56 | tf_op jit(solution)/shard_map/ppermute | solution.py:35
  44.3 4.2 %collective-permute-start.12 = (f32[4]{0:T(128)S(1)}, f32[4]{0:T(128)S(1)}, u32[]{:S(2)}, u32[]{:S(2)}) collective-permute-start(f32[4]{0:T(128)S(1)} %get-tuple-element.43), channel_id=1, source_target_pairs={{0,64},{4,68},{8,72},{12,76},{16,80},{20,84},{24,88},{28,92},{32,9... | collective-permute-start | bytes 56 | tf_op jit(solution)/shard_map/ppermute | solution.py:35
  92.1 22.0 %copy-start.7 = (f32[4,512]{1,0:T(4,128)S(1)}, f32[4,512]{1,0:T(4,128)}, u32[]{:S(2)}) copy-start(f32[4,512]{1,0:T(4,128)} %get-tuple-element.33) | copy-start | bytes 24580
  92.1 11.2 %collective-permute-start.3 = (bf16[4,128,128]{2,1,0:T(8,128)(2,1)}, bf16[4,128,128]{2,1,0:T(8,128)(2,1)S(1)}, u32[]{:S(2)}, u32[]{:S(2)}) collective-permute-start(bf16[4,128,128]{2,1,0:T(8,128)(2,1)} %get-tuple-element.57), channel_id=1, source_target_pairs={{0,4},{4,0},{8,12},{12,8},{16,20},{20,16},{24,28},{28,24},{32,36},... | collective-permute-start | bytes 393224 | tf_op jit(solution)/shard_map/ppermute | solution.py:35
  95.9 21.4 %copy-start.9 = (f32[4]{0:T(128)S(1)}, f32[4]{0:T(128)}, u32[]{:S(2)}) copy-start(f32[4]{0:T(128)} %get-tuple-element.49) | copy-start | bytes 52
  95.9 21.4 %copy-start.10 = (f32[4]{0:T(128)S(1)}, f32[4]{0:T(128)}, u32[]{:S(2)}) copy-start(f32[4]{0:T(128)} %get-tuple-element.56) | copy-start | bytes 52
  95.9 21.4 %copy-start.13 = (f32[4]{0:T(128)S(1)}, f32[4]{0:T(128)}, u32[]{:S(2)}) copy-start(f32[4]{0:T(128)} %get-tuple-element.46) | copy-start | bytes 52
  100.8 24.1 %copy-start.5 = (f32[4,512]{1,0:T(4,128)S(1)}, f32[4,512]{1,0:T(4,128)}, u32[]{:S(2)}) copy-start(f32[4,512]{1,0:T(4,128)} %get-tuple-element.31) | copy-start | bytes 24580
  103.3 25.3 %copy-start.14 = (f32[4]{0:T(128)S(1)}, f32[4]{0:T(128)}, u32[]{:S(2)}) copy-start(f32[4]{0:T(128)} %get-tuple-element.53) | copy-start | bytes 52
  104.0 30.9 %copy-start.4 = (f32[4,512]{1,0:T(4,128)S(1)}, f32[4,512]{1,0:T(4,128)}, u32[]{:S(2)}) copy-start(f32[4,512]{1,0:T(4,128)} %get-tuple-element.30) | copy-start | bytes 24580
  104.0 6.4 %collective-permute-start.5 = (bf16[4,128,128]{2,1,0:T(8,128)(2,1)S(1)}, bf16[4,128,128]{2,1,0:T(8,128)(2,1)S(1)}, u32[]{:S(2)}, u32[]{:S(2)}) collective-permute-start(bf16[4,128,128]{2,1,0:T(8,128)(2,1)S(1)} %fusion.76), channel_id=1, source_target_pairs={{0,8},{4,12},{8,0},{12,4},{16,24},{20,28},{24,16},{28,20},{32,40},... | collective-permute-start | bytes 393224 | tf_op jit(solution)/shard_map/ppermute | solution.py:35
  111.2 6.1 %collective-permute-start.7 = (bf16[4,128,128]{2,1,0:T(8,128)(2,1)S(1)}, bf16[4,128,128]{2,1,0:T(8,128)(2,1)S(1)}, u32[]{:S(2)}, u32[]{:S(2)}) collective-permute-start(bf16[4,128,128]{2,1,0:T(8,128)(2,1)S(1)} %fusion.43), channel_id=1, source_target_pairs={{0,16},{4,20},{8,24},{12,28},{16,0},{20,4},{24,8},{28,12},{32,48},... | collective-permute-start | bytes 393224 | tf_op jit(solution)/shard_map/ppermute | solution.py:35
  117.5 4.1 %collective-permute-start.9 = (bf16[4,128,128]{2,1,0:T(8,128)(2,1)S(1)}, bf16[4,128,128]{2,1,0:T(8,128)(2,1)S(1)}, u32[]{:S(2)}, u32[]{:S(2)}) collective-permute-start(bf16[4,128,128]{2,1,0:T(8,128)(2,1)S(1)} %get-tuple-element.9), channel_id=1, source_target_pairs={{0,32},{4,36},{8,40},{12,44},{16,48},{20,52},{24,56},{28,60},{32,0... | collective-permute-start | bytes 393224 | tf_op jit(solution)/shard_map/ppermute | solution.py:35
  121.8 6.8 %collective-permute-start.11 = (bf16[4,128,128]{2,1,0:T(8,128)(2,1)S(1)}, bf16[4,128,128]{2,1,0:T(8,128)(2,1)S(1)}, u32[]{:S(2)}, u32[]{:S(2)}) collective-permute-start(bf16[4,128,128]{2,1,0:T(8,128)(2,1)S(1)} %fusion.42), channel_id=1, source_target_pairs={{0,64},{4,68},{8,72},{12,76},{16,80},{20,84},{24,88},{28,92},{32,9... | collective-permute-start | bytes 393224 | tf_op jit(solution)/shard_map/ppermute | solution.py:35
  128.7 8.6 %collective-permute-start.13 = (bf16[4,128,128]{2,1,0:T(8,128)(2,1)S(1)}, bf16[4,128,128]{2,1,0:T(8,128)(2,1)S(1)}, u32[]{:S(2)}, u32[]{:S(2)}) collective-permute-start(bf16[4,128,128]{2,1,0:T(8,128)(2,1)S(1)} %fusion.39), channel_id=1, source_target_pairs={{0,128},{4,132},{8,136},{12,140},{16,144},{20,148},{24,152},{28,15... | collective-permute-start | bytes 393224 | tf_op jit(solution)/shard_map/ppermute | solution.py:35
  (8 other events, 86.4 us)
Sparse Core Ops, SparseCore 0:
  146.2 52.8 reduce-scatter.1
